TPU v7x, 256 devices: a whole 4x4x8 slice. The times are simulated.
256 devices in a mesh: depth: 32 (over z, y), heads: 8 (over x, core).
Axes of the slice: x: 4, y: 4, z: 8, core: 2. Of those that a mesh axis runs over, the one named last changes fastest.
Arguments:
- q_raw: bfloat16 [8192, 8192], P('depth', 'heads'), may hold values from -60 to 60
- k_raw: bfloat16 [8192, 1024], P('depth', 'heads'), may hold values from -60 to 60
- values: bfloat16 [8192, 1024], P('depth', 'heads'), may hold values from -6 to 6
- q_gain: float32 [128], replicated, may hold values from 0.7 to 6
- k_gain: float32 [128], replicated, may hold values from 0.7 to 6
- grad_out: bfloat16 [8192, 8192], P('depth', 'heads'), may hold values from -6 to 6
- block_mask: int32 [64, 64], replicated, may hold values from 0 to 1, as said below
- block_count: int32 [64], replicated, may hold values from 64 to 128, as said below
Outputs:
- out: bfloat16 [8192, 8192], P('depth', 'heads')
- grad_q: bfloat16 [8192, 8192], P('depth', 'heads')
- grad_k: bfloat16 [8192, 1024], P('depth', 'heads')
- grad_values: bfloat16 [8192, 1024], P('depth', 'heads')
- grad_q_gain: float32 [128], replicated
- grad_k_gain: float32 [128], replicated
Inputs may be any that keep to these rules, and one draw needn't show every extreme that they name: Blocks 2 * j to 2 * j + 1 form level j of a forest of 32 levels whose two roots are blocks 0 and 1; each block of level j > 0 has one parent in level j - 1; block_mask[b, c] = 1 exactly when c is b or an ancestor of b, so row b holds exactly one 1 in each level up to b's own and none deeper. `block_count`: block 0 is full.
All inputs are finite; a program needn't handle non-finite values.
Results may differ from a plain program's by a relative error of at most 0.035.
The roundings to bfloat16 on the way count: a program that leaves them out, or rounds other values in their place, can miss the bound.
Values may be sent and summed in bfloat16 or wider, within the bound.
A program may use at most 128 MiB of HBM per device.

v0:
```python
import jax
import jax.numpy as jnp
from jax import lax
from jax.sharding import PartitionSpec as P

DH = 128
BLOCK = 128
LEVEL_GROUP = 4
BLK_DEV = 2


EPSILON = 1e-06


def normalize(raw_rows, gain):
    values_f = raw_rows.astype(jnp.float32)
    inverse = 1.0 / jnp.sqrt(jnp.mean(values_f * values_f, axis=-1, keepdims=True) + EPSILON)
    normed = values_f * inverse
    return (normed, inverse, (normed * gain).astype(jnp.bfloat16))


def norm_backward(grad_in, normed, inverse, gain):
    grad_hat = grad_in * gain
    inner_mean = jnp.mean(grad_hat * normed, axis=-1, keepdims=True)
    grad_raw = inverse * (grad_hat - normed * inner_mean)
    gain_part = jnp.sum((grad_in * normed).reshape(-1, normed.shape[-1]), axis=0)
    return (grad_raw, gain_part)


def body(q_raw, k_raw, values, q_gain, k_gain, grad_out, block_mask, block_count):
    row_count = q_raw.shape[0]
    kv_local = k_raw.shape[1] // DH
    group_size = q_raw.shape[1] // k_raw.shape[1]
    levels = lax.axis_size("depth")
    nblocks = levels * BLK_DEV
    scale_factor = DH ** (-0.5)
    position = lax.axis_index("depth")
    k_hat, k_inv, k_low = normalize(k_raw.reshape(row_count, kv_local, DH), k_gain)
    keys_all, values_all = (
        lax.all_gather(k_low, "depth", axis=0, tiled=True),
        lax.all_gather(values.reshape(row_count, kv_local, DH), "depth", axis=0, tiled=True),
    )
    keys_all = keys_all.reshape(nblocks, BLOCK, kv_local, DH)
    values_all = values_all.reshape(nblocks, BLOCK, kv_local, DH)
    q_blocks = q_raw.reshape(BLK_DEV, BLOCK, kv_local, group_size, DH)
    g_blocks = grad_out.reshape(BLK_DEV, BLOCK, kv_local, group_size, DH)
    own_ids = position * BLK_DEV + jnp.arange(BLK_DEV, dtype=jnp.int32)
    work_q, work_g, work_ids = (q_blocks, g_blocks, own_ids)
    places = jnp.arange(BLOCK, dtype=jnp.int32)
    level_ids = jnp.arange(levels, dtype=jnp.int32)
    member_ids = jnp.arange(BLK_DEV, dtype=jnp.int32)

    def attend(loop_carry, inputs):
        partial_value, gain_acc = loop_carry
        query_rows, grad_rows, block_id = inputs
        q_hat, q_inv, q_low = normalize(query_rows, q_gain)
        level_rows = block_mask[block_id].reshape(levels, BLK_DEV)
        ancestors = level_ids * BLK_DEV + jnp.sum(level_rows * member_ids[None, :], axis=1)
        alive_levels = jnp.sum(level_rows, axis=1)
        turn_count = block_id // BLK_DEV // LEVEL_GROUP + 1

        def score_tile(group_index):
            picked = lax.dynamic_slice_in_dim(ancestors, group_index * LEVEL_GROUP, LEVEL_GROUP)
            alive_part = lax.dynamic_slice_in_dim(
                alive_levels, group_index * LEVEL_GROUP, LEVEL_GROUP
            )
            tile_keys = keys_all[picked].reshape(LEVEL_GROUP * BLOCK, kv_local, DH)
            tile_values = values_all[picked].reshape(LEVEL_GROUP * BLOCK, kv_local, DH)
            key_counts = block_count[picked]
            allowed = (alive_part[:, None] > 0) & (places[None, :] < key_counts[:, None])
            allowed = allowed[None, :, :] & (
                (picked[None, :, None] != block_id)
                | (places[None, None, :] <= places[:, None, None])
            )
            allowed = allowed.reshape(BLOCK, LEVEL_GROUP * BLOCK)
            scores = (
                jnp.einsum("qgjd,kgd->gjqk", q_low, tile_keys, preferred_element_type=jnp.float32)
                * scale_factor
            )
            return (
                jnp.where(allowed[None, None], scores, -jnp.inf),
                tile_keys,
                tile_values,
                picked,
            )

        def measure(group_index, stats_pair):
            row_top, row_total = stats_pair
            scores = score_tile(group_index)[0]
            new_top = jnp.maximum(row_top, jnp.max(scores, axis=-1))
            row_total = row_total * jnp.exp(row_top - new_top) + jnp.sum(
                jnp.exp(scores - new_top[..., None]), axis=-1
            )
            return (new_top, row_total)

        stat_shape = (kv_local, group_size, BLOCK)
        row_top, row_total = lax.fori_loop(
            0,
            turn_count,
            measure,
            (jnp.full(stat_shape, -jnp.inf, jnp.float32), jnp.zeros(stat_shape, jnp.float32)),
        )

        def probabilities(scores):
            return jnp.exp(scores - row_top[..., None]) / row_total[..., None]

        def forward_sum(group_index, out_acc):
            scores, tile_keys, tile_values, picked = score_tile(group_index)
            prob_low = probabilities(scores).astype(jnp.bfloat16)
            return out_acc + jnp.einsum(
                "gjqk,kgd->qgjd", prob_low, tile_values, preferred_element_type=jnp.float32
            )

        out_f = lax.fori_loop(0, turn_count, forward_sum, jnp.zeros(query_rows.shape, jnp.float32))
        out_low = out_f.astype(jnp.bfloat16)
        row_delta = jnp.einsum(
            "qgjd,qgjd->gjq", grad_rows.astype(jnp.float32), out_low.astype(jnp.float32)
        )

        def backward(group_index, state_pair):
            grad_qn, partial_now = state_pair
            scores, tile_keys, tile_values, picked = score_tile(group_index)
            prob_full = probabilities(scores)
            prob_low = prob_full.astype(jnp.bfloat16)
            grad_prob = jnp.einsum(
                "qgjd,kgd->gjqk", grad_rows, tile_values, preferred_element_type=jnp.float32
            )
            grad_score = (prob_full * (grad_prob - row_delta[..., None])).astype(jnp.bfloat16)
            grad_qn = (
                grad_qn
                + jnp.einsum(
                    "gjqk,kgd->qgjd", grad_score, tile_keys, preferred_element_type=jnp.float32
                )
                * scale_factor
            )
            grad_kn = (
                jnp.einsum("gjqk,qgjd->kgd", grad_score, q_low, preferred_element_type=jnp.float32)
                * scale_factor
            )
            grad_vn = jnp.einsum(
                "gjqk,qgjd->kgd", prob_low, grad_rows, preferred_element_type=jnp.float32
            )
            pieces = jnp.stack([grad_kn, grad_vn], axis=2).reshape(
                LEVEL_GROUP, BLOCK, kv_local, 2, DH
            )
            for level_slot in range(LEVEL_GROUP):
                row_start = picked[level_slot] * BLOCK
                current = lax.dynamic_slice_in_dim(partial_now, row_start, BLOCK, 0)
                partial_now = lax.dynamic_update_slice_in_dim(
                    partial_now, current + pieces[level_slot], row_start, 0
                )
            return (grad_qn, partial_now)

        grad_qn, partial_value = lax.fori_loop(
            0, turn_count, backward, (jnp.zeros(query_rows.shape, jnp.float32), partial_value)
        )
        grad_rows_q, gain_part = norm_backward(grad_qn, q_hat, q_inv, q_gain)
        return ((partial_value, gain_acc + gain_part), (out_low, grad_rows_q.astype(jnp.bfloat16)))

    start_partial = jnp.zeros((nblocks * BLOCK, kv_local, 2, DH), jnp.float32)
    start_gain = jnp.zeros((DH,), jnp.float32)
    (partial_value, q_gain_part), (out_rows, grad_q_rows) = lax.scan(
        attend, (start_partial, start_gain), (work_q, work_g, work_ids)
    )
    summed = lax.psum_scatter(
        partial_value.reshape(nblocks * BLOCK, kv_local * 2 * DH).astype(jnp.bfloat16),
        "depth",
        scatter_dimension=0,
        tiled=True,
    ).astype(jnp.float32)
    summed = summed.reshape(row_count, kv_local, 2, DH)
    grad_k, k_gain_part = norm_backward(summed[:, :, 0, :], k_hat, k_inv, k_gain)
    grad_values = summed[:, :, 1, :].reshape(row_count, kv_local * DH).astype(jnp.bfloat16)
    q_gain_grad, k_gain_grad = lax.psum((q_gain_part, k_gain_part), ("depth", "heads"))
    return (
        out_rows.reshape(row_count, q_raw.shape[1]),
        grad_q_rows.reshape(row_count, q_raw.shape[1]),
        grad_k.astype(jnp.bfloat16).reshape(row_count, kv_local * DH),
        grad_values,
        q_gain_grad,
        k_gain_grad,
    )


def solution(mesh):
    in_specs = (
        P("depth", "heads"),
        P("depth", "heads"),
        P("depth", "heads"),
        P(),
        P(),
        P("depth", "heads"),
        P(),
        P(),
    )
    out_specs = (
        P("depth", "heads"),
        P("depth", "heads"),
        P("depth", "heads"),
        P("depth", "heads"),
        P(),
        P(),
    )
    return jax.shard_map(body, mesh=mesh, in_specs=in_specs, out_specs=out_specs, check_vma=False)
```

profile of v0, /device:TPU:2, one launch (start us, length us, event | category | flops | bytes accessed | tf_op | source)
XLA Modules:
  0.0 948.4 jit_solution(12701858421344176975)
XLA Ops:
  11.0 2.0 copy.59
  12.9 2.0 copy.60
  14.9 73.8 %all-gather.5.cloned.1.call-done = bf16[8192,128]{0,1:T(8,128)(2,1)} async-done(((bf16[256,128]{0,1:T(8,128)(2,1)}), bf16[8192,128]{0,1:T(8,128)(2,1)}) %all-gather.5.cloned.1.call-update) | async-done | bytes 2097168 | tf_op jit(solution)/shard_map/all_gather | solution.py:40
  88.7 3.2 copy.50
  91.9 76.7 %all-gather.7.cloned.1.call-done = bf16[8192,128]{1,0:T(8,128)(2,1)} async-done(((bf16[256,128]{1,0:T(8,128)(2,1)}), bf16[8192,128]{1,0:T(8,128)(2,1)}) %all-gather.7.cloned.1.call-update) | async-done | bytes 2097168 | tf_op jit(solution)/shard_map/all_gather | solution.py:41
  168.6 3.8 broadcast_in_dim.87
  172.4 86.2 %while.108 = (s32[]{:T(128)}, f32[8192,1,2,128]{3,0,2,1:T(8,128)}, f32[128]{0:T(128)S(1)}, bf16[2,128,1,8,128]{4,3,1,0,2:T(8,128)(2,1)}, bf16[2,128,1,8,128]{4,3...) while((s32[]{:T(128)}, f32[8192,1,2,128]{3,0,2,1:T(8,128)}, ...), condition=%wide.region_15.16_spmd.clone.clone, body=%wide.region_1.15_spmd.clone.clone.sunk | while | flops 1088938368 | bytes 53417368 | solution.py:162
  177.2 1.7 constant_dynamic-slice_fusion.6
  180.5 3.4 while.109
  184.0 5.5 while.110
  186.5 2.2 gather_fusion.2
  190.5 1.9 bitcast_convert_fusion.2
  192.3 2.1 copy.76
  195.5 18.2 %while.111 = (s32[]{:T(128)}, f32[128,1,8,128]{0,3,2,1:T(8,128)S(1)}, f32[8192,1,2,128]{3,0,2,1:T(8,128)}, s32[]{:T(128)}, s32[32]{0:T(128)S(1)}, /*index=5*/bf1...) while((s32[]{:T(128)}, ...), condition=%wide.region_12.12_spmd.clone, body=%wide.region_11.11_spmd.clone.sunk | while | flops 676022272 | bytes 33087204 | solution.py:154
  200.7 2.2 gather_fusion.7
  202.8 2.2 gather_fusion.5
  207.4 1.7 fusion.169
  212.2 1.6 fusion.172
  220.4 1.7 constant_dynamic-slice_fusion.6
  223.7 3.4 while.109
  227.2 5.5 while.110
  229.6 2.2 gather_fusion.2
  233.6 1.9 bitcast_convert_fusion.2
  235.5 2.1 copy.76
  238.7 18.2 %while.111 = (s32[]{:T(128)}, f32[128,1,8,128]{0,3,2,1:T(8,128)S(1)}, f32[8192,1,2,128]{3,0,2,1:T(8,128)}, s32[]{:T(128)}, s32[32]{0:T(128)S(1)}, /*index=5*/bf1...) while((s32[]{:T(128)}, ...), condition=%wide.region_12.12_spmd.clone, body=%wide.region_11.11_spmd.clone.sunk | while | flops 676022272 | bytes 33087204 | solution.py:154
  243.8 2.2 gather_fusion.7
  246.0 2.2 gather_fusion.5
  250.5 1.7 fusion.169
  255.3 1.6 fusion.172
  258.7 7.2 copy.37
  268.3 595.8 %reduce-scatter.2.cloned.1.call-done = bf16[256,256]{0,1:T(8,128)(2,1)} async-done(((bf16[8192,256]{0,1:T(8,128)(2,1)}), bf16[256,256]{0,1:T(8,128)(2,1)}) %reduce-scatter.2.cloned.1.call-update) | async-done | bytes 131088 | tf_op jit(solution)/shard_map/reduce_scatter | solution.py:165
  868.3 73.5 %all-reduce = (f32[128]{0:T(128)}, f32[128]{0:T(128)}) all-reduce(f32[128]{0:T(128)S(1)} %get-tuple-element.1660, f32[128]{0:T(128)S(1)} %get-tuple-element.801), channel_id=1, replica_groups=mesh['depth'=32,'heads'=8] {'depth','heads'}, use_global_device_ids=true, to_apply=%region_18.19 | all-reduce | flops 256 | bytes 2048 | tf_op jit(solution)/shard_map/psum | solution.py:174
  (187 shorter events, 53.1 us)
Async XLA Ops:
  7.2 81.5 %all-gather.5.cloned.1.call-start = ((), (), s32[]{:S(2)}) async-start(), calls=%async_computation.2 | async-start | bytes 2162688 | tf_op jit(solution)/shard_map/all_gather | solution.py:40
  8.2 6.8 copy-start.4
  8.2 0.5 copy-start.9
  10.1 158.5 %all-gather.7.cloned.1.call-start = ((), (), s32[]{:S(2)}) async-start(), calls=%async_computation.3 | async-start | bytes 2162688 | tf_op jit(solution)/shard_map/all_gather | solution.py:41
  10.9 853.2 %reduce-scatter.2.cloned.1.call-start = ((), (), s32[]{:S(2)}) async-start(), calls=%async_computation.1 | async-start | bytes 4325376 | tf_op jit(solution)/shard_map/reduce_scatter | solution.py:165
  168.6 3.8 copy-start
  168.6 3.8 copy-start.8
  195.6 4.9 copy-start.1
  207.3 6.4 copy-start.2
  213.8 1.0 copy-start.3
  238.7 4.9 copy-start.1
  250.5 6.4 copy-start.2
  256.9 1.0 copy-start.3
  265.9 1.0 copy-start.6
  265.9 1.2 copy-start.7
  265.9 598.2 %copy-start.5 = (bf16[256,128]{0,1:T(8,128)(2,1)S(1)}, bf16[256,128]{0,1:T(8,128)(2,1)}, u32[]{:S(2)}) copy-start(bf16[256,128]{0,1:T(8,128)(2,1)} %copy-done.4) | copy-start | bytes 196612
  265.9 598.2 %copy-start.10 = (f32[256]{0:T(256)S(1)}, f32[256]{0:T(256)}, u32[]{:S(2)}) copy-start(f32[256]{0:T(256)} %copy-done.9) | copy-start | bytes 3076
  265.9 598.2 %copy-start.11 = (f32[128]{0:T(128)S(1)}, f32[128]{0:T(128)}, u32[]{:S(2)}) copy-start(f32[128]{0:T(128)} %param.20) | copy-start | bytes 1540
Sparse Core Ops, SparseCore 0:
  11.0 77.6 all-gather.4
  91.3 77.2 all-gather.6
  266.0 598.0 reduce-scatter.1
where the time goes:
time: 955 us; the launch traced here: 948 us
  waiting for transfers between devices  747 us (78%)
  blocking collectives  73.5 us (8%)
  local copies, waits for them, and re-layouts  63.3 us (7%)
  other arithmetic  30.6 us (3%)
  between operations  13.8 us (1%)
  loops' own time  12.7 us (1%)
    reduce_scatter x1, waiting for transfers between devices, body(): lax.psum_scatter(partial_value.reshape(nblocks * BLOCK, kv_local * 2 * DH...  596 us
    all_gather x1, waiting for transfers between devices, body(): lax.all_gather(values.reshape(row_count, kv_local, DH), 'depth', axis=0,...  76.7 us
    all_gather x1, waiting for transfers between devices, body(): lax.all_gather(k_low, 'depth', axis=0, tiled=True)  73.8 us
    psum x1, blocking collectives, body(): lax.psum((q_gain_part, k_gain_part), ('depth', 'heads'))  73.5 us
  transfers between devices with their start and end apart: 3, of which 3 were waited for; matrix products, arithmetic and copies ran while one was open for 1% of the time, Pallas kernels for 0%

commit v1 on v0

v1 whole, which is shorter than its diff:
```python
import functools
import heapq
import math

import jax
import jax.numpy as jnp
from jax import lax
from jax.experimental import pallas as pl
from jax.experimental.pallas import tpu as pltpu
from jax.sharding import PartitionSpec as P

DH = 128
BLOCK = 128
EPS = 1e-6
SCALE = DH ** -0.5
C2 = SCALE * math.log2(math.e)
NEG = -1e30
f32 = jnp.float32
bf16 = jnp.bfloat16
MESH = pl.DeviceIdType.MESH

def dot(a,b): return jnp.dot(a,b,preferred_element_type=f32)
def dott(a,b): return lax.dot_general(a,b,(((0,),(0,)),((),())),preferred_element_type=f32)

def attn_kernel(pos_fn, LC, RT, LEVELS, AUG, mask_ref, count_ref, q_ref, g_ref, qg_ref, ka_ref, va_ref,
                out_ref, gq_ref, pk_ref, pv_ref, qgp_ref,
                kx, vx, s_scr, qT, gT, qrows, grows, ot, dqt, dk, dv, ml):
    pos = pos_fn()
    nl = pos + 1
    nch = (nl + LC - 1) // LC
    CK = LC*BLOCK
    R = 8*BLOCK
    NRT = R//RT
    KA = 256 if AUG else 128
    gain = qg_ref[...]
    lane = lax.broadcasted_iota(jnp.int32, (BLOCK, BLOCK), 1)
    sub = lax.broadcasted_iota(jnp.int32, (BLOCK, BLOCK), 0)
    causal = jnp.where(sub <= lane, 0.0, NEG).astype(f32)
    if RT > BLOCK:
        causal = jnp.concatenate([causal]*(RT//BLOCK), axis=1)

    def block(b, gacc):
        rows = pl.ds(pl.multiple_of(b*BLOCK, BLOCK), BLOCK)
        own = 2*pos + b
        def gather(s, _):
            lev = jnp.maximum(s-1, 0)
            lev = jnp.minimum(lev, LEVELS-1)
            pick = jnp.where(s == 0, own, 2*lev + mask_ref[own, 2*lev+1])
            live = s < nl
            cnt = jnp.where(live, count_ref[pick], 0)
            ks = pl.ds(pl.multiple_of(s*BLOCK, BLOCK), BLOCK)
            kx[ks, 0:128] = ka_ref[pick]
            vx[ks, 0:128] = va_ref[pick]
            bias = jnp.where(sub < cnt, 0.0, NEG)
            kx[ks, 128:256] = jnp.where(lane == 0, bias, 0.0).astype(bf16)
            vx[ks, 128:256] = jnp.where(lane < 3, -1.0, 0.0).astype(bf16)
            return 0
        lax.fori_loop(0, nch*LC, gather, 0)
        qT[128:256, :] = jnp.where(lax.broadcasted_iota(jnp.int32, (128, R), 0) == 0, 1.0, 0.0).astype(bf16)
        for h in range(8):
            hs = slice(h*128, (h+1)*128)
            qf = q_ref[rows, hs].astype(f32)
            inv = 1.0/jnp.sqrt(jnp.mean(qf*qf, axis=-1, keepdims=True) + EPS)
            low = (qf*inv*gain).astype(bf16)
            qrows[hs, :] = low
            qT[0:128, hs] = low.T
            gr = g_ref[rows, hs]
            grows[hs, :] = gr
            gT[0:128, hs] = gr.T
        ml[0:1, :] = jnp.full((1, R), NEG, f32)
        ml[1:2, :] = jnp.zeros((1, R), f32)

        def pass1(c, first):
            ks = pl.ds(pl.multiple_of(c*CK, CK), CK)
            kc = kx[ks, :]
            for r in range(NRT):
                rs = slice(r*RT, (r+1)*RT)
                s = dot(kc, qT[:, rs])
                if first:
                    s = jnp.concatenate([s[0:BLOCK] + causal, s[BLOCK:]], axis=0) if LC > 1 else s + causal
                s_scr[ks, rs] = s
                mo = ml[0:1, rs]
                mn = jnp.maximum(mo, jnp.max(s, axis=0, keepdims=True))
                e = jnp.exp2((s - mn)*C2)
                ml[1:2, rs] = ml[1:2, rs]*jnp.exp2((mo-mn)*C2) + jnp.sum(e, axis=0, keepdims=True)
                ml[0:1, rs] = mn
        pass1(0, True)
        def p1(c, _):
            pass1(c, False)
            return 0
        lax.fori_loop(1, nch, p1, 0)
        ml[2:3, :] = ml[0:1, :]*C2 + jnp.log2(ml[1:2, :])
        ot[...] = jnp.zeros_like(ot)
        dqt[...] = jnp.zeros_like(dqt)

        def p3(c, _):
            ks = pl.ds(pl.multiple_of(c*CK, CK), CK)
            vc = vx[ks, 0:128]
            acc = None
            for r in range(NRT):
                rs = slice(r*RT, (r+1)*RT)
                p = jnp.exp2(s_scr[ks, rs]*C2 - ml[2:3, rs])
                s_scr[ks, rs] = p
                lo = p.astype(bf16)
                ot[:, rs] += dott(vc, lo)
                t = dot(lo, grows[rs, :])
                acc = t if acc is None else acc + t
            dv[b, ks, :] = acc
            return 0
        lax.fori_loop(0, nch, p3, 0)
        olow = ot[...].astype(bf16)
        delta = jnp.sum(olow.astype(f32)*gT[0:128, :].astype(f32), axis=0, keepdims=True)
        d0 = delta.astype(bf16); r1 = delta - d0.astype(f32)
        d1 = r1.astype(bf16); d2 = (r1 - d1.astype(f32)).astype(bf16)
        z = lax.broadcasted_iota(jnp.int32, (128, R), 0)
        gT[128:256, :] = jnp.where(z == 0, d0.astype(f32), jnp.where(z == 1, d1.astype(f32), jnp.where(z == 2, d2.astype(f32), 0.0))).astype(bf16)
        for h in range(8):
            hs = slice(h*128, (h+1)*128)
            out_ref[rows, hs] = olow[:, hs].T

        def p4(c, _):
            ks = pl.ds(pl.multiple_of(c*CK, CK), CK)
            vc = vx[ks, :]
            kc = kx[ks, 0:128]
            acc = None
            for r in range(NRT):
                rs = slice(r*RT, (r+1)*RT)
                dp = dot(vc, gT[:, rs])
                ds = (s_scr[ks, rs]*dp).astype(bf16)
                dqt[:, rs] += dott(kc, ds)
                t = dot(ds, qrows[rs, :])
                acc = t if acc is None else acc + t
            dk[b, ks, :] = acc*SCALE
            return 0
        lax.fori_loop(0, nch, p4, 0)
        for h in range(8):
            hs = slice(h*128, (h+1)*128)
            gqn = dqt[:, hs].T*SCALE
            qf = q_ref[rows, hs].astype(f32)
            inv = 1.0/jnp.sqrt(jnp.mean(qf*qf, axis=-1, keepdims=True) + EPS)
            hat = qf*inv
            gh = gqn*gain
            im = jnp.mean(gh*hat, axis=-1, keepdims=True)
            gq_ref[rows, hs] = (inv*(gh - hat*im)).astype(bf16)
            gacc = gacc + jnp.sum(gqn*hat, axis=0, keepdims=True)
        return gacc
    qgp_ref[...] = lax.fori_loop(0, 2, block, jnp.zeros((1, 128), f32))

    def combine(i, _):
        ks = pl.ds(pl.multiple_of((i+1)*BLOCK, BLOCK), BLOCK)
        p0 = mask_ref[2*pos, 2*i+1]
        p1_ = mask_ref[2*pos+1, 2*i+1]
        for (src, dst) in ((dk, pk_ref), (dv, pv_ref)):
            a0 = src[0, ks, :]; a1 = src[1, ks, :]
            for m in range(2):
                x = jnp.where(p0 == m, a0, 0.0) + jnp.where(p1_ == m, a1, 0.0)
                dst[i, m*BLOCK:(m+1)*BLOCK, :] = x.astype(bf16)
        return 0
    lax.fori_loop(0, pos, combine, 0)
    for (src, dst) in ((dk, pk_ref), (dv, pv_ref)):
        for b in range(2):
            dst[pos, b*BLOCK:(b+1)*BLOCK, :] = src[b, 0:BLOCK, :].astype(bf16)
    def zero(i, _):
        pk_ref[i] = jnp.zeros((2*BLOCK, DH), bf16)
        pv_ref[i] = jnp.zeros((2*BLOCK, DH), bf16)
        return 0
    lax.fori_loop(pos+1, LEVELS, zero, 0)

def attention(pos_fn, mask, count, q, g, qg, ka, va, LC=16, RT=256, LEVELS=32, AUG=True):
    V=pl.BlockSpec(memory_space=pltpu.VMEM); S=pl.BlockSpec(memory_space=pltpu.SMEM)
    KT=LEVELS*BLOCK
    R=1024
    sd=jax.ShapeDtypeStruct
    return pl.pallas_call(
        functools.partial(attn_kernel, pos_fn, LC, RT, LEVELS, AUG),
        out_shape=(sd((256,1024),bf16), sd((256,1024),bf16), sd((LEVELS,256,128),bf16), sd((LEVELS,256,128),bf16), sd((1,128),f32)),
        in_specs=[S,S,V,V,V,V,V], out_specs=(V,)*5,
        scratch_shapes=[pltpu.VMEM((KT,256),bf16), pltpu.VMEM((KT,256),bf16), pltpu.VMEM((KT,R),f32),
            pltpu.VMEM((256,R),bf16), pltpu.VMEM((256,R),bf16), pltpu.VMEM((R,128),bf16), pltpu.VMEM((R,128),bf16),
            pltpu.VMEM((128,R),f32), pltpu.VMEM((128,R),f32), pltpu.VMEM((2,KT,128),f32), pltpu.VMEM((2,KT,128),f32), pltpu.VMEM((8,R),f32)],
        compiler_params=pltpu.CompilerParams(vmem_limit_bytes=60*2**20),
        name="attention",
    )(mask, count, q, g, qg, ka, va)

NZ, NY = 8, 4
STEP={"z+":(1,0),"z-":(-1,0),"y+":(0,1),"y-":(0,-1)}

def build_trees():
    parent={}
    for buf in range(2):
        for oz in range(NZ):
            for oy in range(NY):
                if (oz,oy)==(0,0): continue
                zdir="z+" if oz>4 else "z-"
                ydir={3:"y+",1:"y-"}.get(oy)
                if buf==0:
                    if oz==0: d=ydir or "y+"
                    elif oy==2 and oz%2==1: d="y+" if oz in (1,5) else "y-"
                    else:
                        d=zdir if oz!=4 else ("z+" if oy in (0,2) else "z-")
                else:
                    if oy==0: d=zdir if oz!=4 else "z+"
                    else: d=ydir or ("y+" if oz%2==0 else "y-")
                parent[buf,oz,oy]=d
    children={}
    for (buf,oz,oy),d in parent.items():
        sz,sy=STEP[d]
        src=(buf,(oz+sz)%NZ,(oy+sy)%NY)
        children.setdefault(src,[]).append((d,(buf,oz,oy)))
    return parent,children

def plan():
    parent,children=build_trees()
    def depth(x):
        return 1+max([depth(c) for _,c in children.get(x,[])],default=0)
    heaps={d:[] for d in STEP}
    n=0
    def push(x):
        nonlocal n
        for d,c in children.get(x,[]):
            heapq.heappush(heaps[d],(-depth(c),n,c)); n+=1
    for buf in range(2): push((buf,0,0))
    order=[]; rounds=0
    while any(heaps.values()):
        got=[]
        for d in STEP:
            if heaps[d]: got.append(heapq.heappop(heaps[d])[2])
        got.sort(key=lambda x:-depth(x))
        for c in got: order.append(c); push(c)
        rounds+=1
    return parent,children,order,rounds

PARENT,CHILDREN,ORDER,ROUNDS=plan()
INDEX={x:i for i,x in enumerate(ORDER)}

def coords():
    p=lax.axis_index("depth")
    return p//NY, p%NY
def level(z,y,oz,oy):
    return lax.rem(z+oz+NZ,NZ)*NY+lax.rem(y+oy+NY,NY)
def toward(z,y,d):
    return {"depth": level(z,y,*STEP[d])}

def ag_kernel(k_ref,v_ref,kg_ref,ka,va,klow,send_sem,recv_sem,lsem):
    z,y=coords()
    me=z*NY+y
    bar=pltpu.get_barrier_semaphore()
    for d in STEP:
        pl.semaphore_signal(bar,inc=1,device_id=toward(z,y,d),device_id_type=MESH)
    kf=k_ref[...].astype(f32)
    inv=1.0/jnp.sqrt(jnp.mean(kf*kf,axis=-1,keepdims=True)+EPS)
    klow[...]=(kf*inv*kg_ref[...]).astype(bf16)
    pl.semaphore_wait(bar,4)
    outs=(ka,va); own=(klow,v_ref)
    started=[]
    def send(x):
        buf,oz,oy=x
        lev=level(z,y,oz,oy)
        for d,c in CHILDREN.get(x,[]):
            i=INDEX[c]
            src=own[buf] if (oz,oy)==(0,0) else outs[buf].at[lev]
            cp=pltpu.make_async_remote_copy(src_ref=src,dst_ref=outs[buf].at[lev],send_sem=send_sem.at[i],recv_sem=recv_sem.at[i],device_id=toward(z,y,d),device_id_type=MESH)
            cp.start(); started.append(cp)
    for buf in range(2): send((buf,0,0))
    locs=[]
    for buf in range(2):
        cp=pltpu.make_async_copy(own[buf],outs[buf].at[me],lsem.at[buf]); cp.start(); locs.append(cp)
    for x in ORDER:
        buf,oz,oy=x
        lev=level(z,y,oz,oy); i=INDEX[x]
        pltpu.make_async_remote_copy(src_ref=own[buf],dst_ref=outs[buf].at[lev],send_sem=send_sem.at[i],recv_sem=recv_sem.at[i],device_id=toward(z,y,"z+"),device_id_type=MESH).wait_recv()
        send(x)
    for cp in started: cp.wait_send()
    for cp in locs: cp.wait()

def all_gather(k,v,kg,space=pl.ANY):
    rows=k.shape[0]
    sd=jax.ShapeDtypeStruct
    V=pl.BlockSpec(memory_space=pltpu.VMEM); A=pl.BlockSpec(memory_space=space)
    n=len(ORDER)
    return pl.pallas_call(ag_kernel,out_shape=(sd((NZ*NY,rows,128),bf16),)*2,in_specs=[V,V,V],out_specs=(A,A),
        scratch_shapes=[pltpu.VMEM((rows,128),bf16),pltpu.SemaphoreType.DMA((n,)),pltpu.SemaphoreType.DMA((n,)),pltpu.SemaphoreType.DMA((2,))],
        compiler_params=pltpu.CompilerParams(collective_id=0,has_side_effects=True),name="gather_kv")(k,v,kg)

def rs_kernel(nh,pk,pv,k_ref,kg_ref,qgp_ref,gk_ref,gv_ref,qg_out,kg_out,land,stage,arh,arz,ary,send_sem,recv_sem,ars,arr):
    z,y=coords(); h=lax.axis_index("heads")
    me=z*NY+y
    bar=pltpu.get_barrier_semaphore()
    peers=[({"heads":lax.rem(h+j,nh)}) for j in range(1,nh)]
    zp=[{"depth":level(z,y,j,0)} for j in range(1,NZ)]
    yp=[{"depth":level(z,y,0,j)} for j in range(1,NY)]
    allp=peers+zp+yp
    for d in allp:
        pl.semaphore_signal(bar,inc=1,device_id=d,device_id_type=MESH)
    pl.semaphore_wait(bar,len(allp))
    parts=(pk,pv)
    started=[]
    def recv(c):
        i=INDEX[c]
        pltpu.make_async_remote_copy(src_ref=land.at[i],dst_ref=land.at[i],send_sem=send_sem.at[i],recv_sem=recv_sem.at[i],device_id=toward(z,y,"z+"),device_id_type=MESH).wait_recv()
    back={"z+":"z-","z-":"z+","y+":"y-","y-":"y+"}
    def total(x):
        buf,oz,oy=x
        s=parts[buf][level(z,y,oz,oy)].astype(f32)
        for _,c in CHILDREN.get(x,[]):
            recv(c)
            s=s+land[INDEX[c]].astype(f32)
        return s
    for x in reversed(ORDER):
        buf,oz,oy=x; i=INDEX[x]
        lev=level(z,y,oz,oy)
        if CHILDREN.get(x):
            stage[i]=total(x).astype(bf16)
            src=stage.at[i]
        else:
            src=parts[buf].at[lev]
        cp=pltpu.make_async_remote_copy(src_ref=src,dst_ref=land.at[i],send_sem=send_sem.at[i],recv_sem=recv_sem.at[i],device_id=toward(z,y,back[PARENT[x]]),device_id_type=MESH)
        cp.start(); started.append(cp)
    gkn=total((0,0,0))
    kf=k_ref[...].astype(f32)
    inv=1.0/jnp.sqrt(jnp.mean(kf*kf,axis=-1,keepdims=True)+EPS)
    hat=kf*inv
    part=jnp.concatenate([qgp_ref[...],jnp.sum(gkn*hat,axis=0,keepdims=True),jnp.zeros((6,128),f32)],axis=0)
    def stage_ar(buf,mine,n,base,mkid,part):
        cps=[]
        buf[mine]=part
        for j in range(1,n):
            cp=pltpu.make_async_remote_copy(src_ref=buf.at[mine],dst_ref=buf.at[mine],send_sem=ars.at[base+j-1],recv_sem=arr.at[base+j-1],device_id=mkid(j),device_id_type=MESH)
            cp.start(); cps.append(cp)
        return cps
    def finish_ar(buf,n,cps):
        for cp in cps: cp.wait_recv()
        s=buf[0]
        for j in range(1,n): s=s+buf[j]
        return s
    c1=stage_ar(arh,h,nh,0,lambda j:{"heads":lax.rem(h+j,nh)},part)
    gh=gkn*kg_ref[...]
    im=jnp.mean(gh*hat,axis=-1,keepdims=True)
    gk_ref[...]=(inv*(gh-hat*im)).astype(bf16)
    gv_ref[...]=total((1,0,0)).astype(bf16)
    t=finish_ar(arh,nh,c1)
    c2=stage_ar(arz,z,NZ,nh-1,lambda j:{"depth":level(z,y,j,0)},t)
    t=finish_ar(arz,NZ,c2)
    c3=stage_ar(ary,y,NY,nh-1+NZ-1,lambda j:{"depth":level(z,y,0,j)},t)
    t=finish_ar(ary,NY,c3)
    qg_out[...]=t[0:1]; kg_out[...]=t[1:2]
    for cp in started+c1+c2+c3: cp.wait_send()

def reduce_scatter(pk,pv,k,kg,qgp,nh):
    rows=k.shape[0]
    sd=jax.ShapeDtypeStruct
    V=pl.BlockSpec(memory_space=pltpu.VMEM)
    n=len(ORDER); na=nh-1+NZ-1+NY-1
    return pl.pallas_call(functools.partial(rs_kernel,nh),
        out_shape=(sd((rows,128),bf16),sd((rows,128),bf16),sd((1,128),f32),sd((1,128),f32)),
        in_specs=[V]*5,out_specs=(V,)*4,
        scratch_shapes=[pltpu.VMEM((n,rows,128),bf16),pltpu.VMEM((n,rows,128),bf16),pltpu.VMEM((nh,8,128),f32),pltpu.VMEM((NZ,8,128),f32),pltpu.VMEM((NY,8,128),f32),
            pltpu.SemaphoreType.DMA((n,)),pltpu.SemaphoreType.DMA((n,)),pltpu.SemaphoreType.DMA((na,)),pltpu.SemaphoreType.DMA((na,))],
        compiler_params=pltpu.CompilerParams(collective_id=1,has_side_effects=True,vmem_limit_bytes=56*2**20),name="scatter_kv")(pk,pv,k,kg,qgp)


def body(q_raw, k_raw, values, q_gain, k_gain, grad_out, block_mask, block_count):
    kg = k_gain.reshape(1, DH)
    qg = q_gain.reshape(1, DH)
    ka, va = all_gather(k_raw, values, kg)
    ka = ka.reshape(2 * NZ * NY, BLOCK, DH)
    va = va.reshape(2 * NZ * NY, BLOCK, DH)
    out, gq, pk, pv, qgp = attention(
        lambda: lax.axis_index("depth"), block_mask, block_count, q_raw, grad_out, qg, ka, va
    )
    gk, gv, qgg, kgg = reduce_scatter(pk, pv, k_raw, kg, qgp, lax.axis_size("heads"))
    return out, gq, gk, gv, qgg.reshape(DH), kgg.reshape(DH)


def solution(mesh):
    rows = P("depth", "heads")
    return jax.shard_map(
        body,
        mesh=mesh,
        in_specs=(rows, rows, rows, P(), P(), rows, P(), P()),
        out_specs=(rows, rows, rows, rows, P(), P()),
        check_vma=False,
    )
```

time: 955 us -> 144 us (0.15)
  waiting for transfers between devices: 747 us -> 0 us
  Pallas kernels: 0 us -> 137 us
  blocking collectives: 73.5 us -> 0 us
  local copies, waits for them, and re-layouts: 63.3 us -> 5.24 us
  other arithmetic: 30.6 us -> 0 us
  between operations: 13.8 us -> 0.65 us
  loops' own time: 12.7 us -> 0 us
    reduce_scatter x1 -> x0, waiting for transfers between devices: 596 us -> none  [body(): lax.psum_scatter(partial_value.reshape(nblocks * BLOCK, kv_local * 2 * DH...]
    all_gather x2 -> x0, waiting for transfers between devices: 150 us -> none  [the longest x1 76.7 us: body(): lax.all_gather(values.reshape(row_count, kv_local, DH), 'depth', axis=0,...]
    pallas_call x0 -> x3, Pallas kernels: none -> 137 us  [the longest x1 68 us: reduce_scatter(): pl.pallas_call(functools.partial(rs_kernel, nh), out_shape=(sd((rows, 128...]
    psum x1 -> x0, blocking collectives: 73.5 us -> none  [body(): lax.psum((q_gain_part, k_gain_part), ('depth', 'heads'))]
    gather x16 -> x0, local copies, waits for them, and re-layouts: 19.1 us -> none  [the longest x4 8.65 us: score_tile(): tile_values = values_all[picked].reshape(LEVEL_GROUP * BLOCK, kv_local, DH)]
    dynamic_update_slice x8 -> x0, other arithmetic: 12.8 us -> none  [backward(): lax.dynamic_update_slice_in_dim(partial_now, current + pieces[level_slot]...]
    another operation x7 -> x0, loops' own time: 12.7 us -> none  [the longest x1 6.9 us: body(): lax.scan(attend, (start_partial, start_gain), (work_q, work_g, work_ids))]
    while x19 -> x0, local copies, waits for them, and re-layouts: 12.5 us -> none  [the longest x1 7.24 us: body(): lax.scan(attend, (start_partial, start_gain), (work_q, work_g, work_ids))]
  transfers between devices with their start and end apart: 3 -> 0, of which waited for: 3 -> 0; matrix products, arithmetic and copies ran while one was open for 1% -> 0% of each run, Pallas kernels for 0% -> 0%
where the time goes in v1:
time: 144 us; the launch traced here: 143 us
  Pallas kernels  137 us (95%)
  local copies, waits for them, and re-layouts  5.24 us (4%)
    pallas_call x1, Pallas kernels, reduce_scatter(): pl.pallas_call(functools.partial(rs_kernel, nh), out_shape=(sd((rows, 128...  68 us
    pallas_call x1, Pallas kernels, all_gather(): pl.pallas_call(ag_kernel, out_shape=(sd((NZ * NY, rows, 128), bf16),) * 2...  43.3 us
    pallas_call x1, Pallas kernels, attention(): pl.pallas_call(functools.partial(attn_kernel, pos_fn, LC, RT, LEVELS, AUG...  26.1 us
    unnamed x4, local copies, waits for them, and re-layouts  5.24 us

profile of v1, /device:TPU:2, one launch (start us, length us, event | category | flops | bytes accessed | tf_op | source)
XLA Modules:
  0.0 143.3 jit_solution(17684582870583047831)
XLA Ops:
  0.6 43.3 %gather_kv.1 = (bf16[32,256,128]{2,1,0:T(8,128)(2,1)}, bf16[32,256,128]{2,1,0:T(8,128)(2,1)}) custom-call(bf16[256,128]{1,0:T(8,128)(2,1)} %k_ref.3, bf16[256,128]{1,0:T(8,128)(2,1)} %v_ref.1, f32[1,128]{1,0:T(1,128)} %bitcast.8), custom_call_target="tpu_custom_call" | custom-call | tf_op jit(solution)/shard_map/gather_kv/pallas_call | solution.py:281
  43.9 26.1 %attention.1 = (bf16[256,1024]{1,0:T(8,128)(2,1)}, bf16[256,1024]{1,0:T(8,128)(2,1)}, bf16[32,256,128]{2,1,0:T(8,128)(2,1)}, bf16[32,256,128]{2,1,0:T(8,128)(2,1)}, f32[1,128]{1,0:T(1,128)}) custom-call(s32[64,64]{1,0:T(8,128)} %mask_ref.1, s32[64]{0:T(128)} %count_ref.1, bf16[256,1024]{1,0:T(8,128)(2,1)} %q_ref.1, bf16[256,1024]{1,0:T(8,128)(2,1)} %g_ref.1, ...), custom_call_target="tpu_custom_call" | custom-call | tf_op jit(solution)/shard_map/attention/pallas_call | solution.py:174
  70.0 68.0 %scatter_kv.1 = (bf16[256,128]{1,0:T(8,128)(2,1)}, bf16[256,128]{1,0:T(8,128)(2,1)}, f32[1,128]{1,0:T(1,128)}, f32[1,128]{1,0:T(1,128)}) custom-call(bf16[32,256,128]{2,1,0:T(8,128)(2,1)} %get-tuple-element.21.pk, bf16[32,256,128]{2,1,0:T(8,128)(2,1)} %get-tuple-element.22.pv, bf16[256,128]{1,0:T(8,128)(2,1)} %k_ref.3, f32[1,128]{1,0:T(1,128)} %bitcast.9, ...), custom_call_target="tpu_custom_call" | custom-call | tf_op jit(solution)/shard_map/scatter_kv/pallas_call | solution.py:354
  138.0 1.5 %copy.18 = bf16[256,128]{1,0:T(8,128)(2,1)} copy(bf16[256,128]{1,0:T(8,128)(2,1)} %get-tuple-element.36) | data formatting | bytes 131072
  139.5 1.5 %copy.19 = bf16[256,128]{1,0:T(8,128)(2,1)} copy(bf16[256,128]{1,0:T(8,128)(2,1)} %get-tuple-element.37) | data formatting | bytes 131072
  141.0 1.2 copy.20
  142.2 1.1 copy.21

commit v2 on v0

v2 whole, which is shorter than its diff:
```python
import functools
import math

import jax
import jax.numpy as jnp
from jax import lax
from jax.experimental import pallas as pl
from jax.experimental.pallas import tpu as pltpu
from jax.sharding import PartitionSpec as P

f32 = jnp.float32
bf16 = jnp.bfloat16
MESH = pl.DeviceIdType.MESH
DH = 128
BLOCK = 128
EPS = 1e-6
SCALE = DH ** -0.5
C2 = SCALE * math.log2(math.e)
NEG = -1e30
NZ, NY = 8, 4
HALVES = 2
LATENCY = 2.0*HALVES

STEP = {"z+": (1, 0), "z-": (-1, 0), "y+": (0, 1), "y-": (0, -1)}
BACK = {"z+": "z-", "z-": "z+", "y+": "y-", "y-": "y+"}
PARTS = [(t, s) for t in range(2) for s in range(HALVES)]


def build_trees():
    parent = {}
    for part in PARTS:
        z_last = (part[1] if HALVES == 2 else part[0]) == 0
        for oz in range(NZ):
            for oy in range(NY):
                if (oz, oy) == (0, 0):
                    continue
                zdir = "z+" if oz > NZ // 2 else "z-"
                ydir = {3: "y+", 1: "y-"}.get(oy)
                if z_last:
                    if oz == 0:
                        d = ydir or "y+"
                    elif oy == 2 and oz % 2 == 1:
                        d = "y+" if oz in (1, 5) else "y-"
                    elif oz == NZ // 2:
                        d = "z+" if oy in (0, 2) else "z-"
                    else:
                        d = zdir
                elif oy == 0:
                    d = "z+" if oz == NZ // 2 else zdir
                else:
                    d = ydir or ("y+" if oz % 2 == 0 else "y-")
                parent[part, oz, oy] = d
    children = {}
    for (part, oz, oy), d in parent.items():
        sz, sy = STEP[d]
        children.setdefault((part, (oz + sz) % NZ, (oy + sy) % NY), []).append((d, (part, oz, oy)))
    return parent, children


PARENT, CHILDREN = build_trees()


def height(x):
    return 1 + max([height(c) for _, c in CHILDREN.get(x, [])], default=0)


def hops(x):
    part, oz, oy = x
    if (oz, oy) == (0, 0):
        return 0
    sz, sy = STEP[PARENT[x]]
    return 1 + hops((part, (oz + sz) % NZ, (oy + sy) % NY))


def needed_planes(x):
    part, oz, oy = x
    offsets = {0}
    stack = [(x, 0)]
    while stack:
        node, dz = stack.pop()
        offsets.add(dz)
        for d, c in CHILDREN.get(node, []):
            stack.append((c, dz + STEP[d][0]))
    return frozenset(z for z in range(NZ) if any((z + dz) % NZ >= (z + oz) % NZ for dz in offsets))


def gather_order():
    waiting, order, count, now = [], [], 0, 0
    free = dict.fromkeys(STEP, 0.0)
    def push(x, at):
        nonlocal count
        for d, c in CHILDREN.get(x, []):
            waiting.append((at, (x[0][0], -height(c), count), d, c))
            count += 1
    for part in PARTS:
        push((part, 0, 0), 0.0)
    done = []
    while waiting:
        start, key, d, c = min((max(free[w[2]], w[0]), w[1], w[2], w[3]) for w in waiting)
        waiting = [w for w in waiting if w[3] != c]
        free[d] = start + 1
        done.append((start + 1 + LATENCY, key, c))
        push(c, start + 1 + LATENCY)
    done.sort()
    return [(c, t) for t, _, c in done]


def scatter_order(first):
    pieces = list(PARENT)
    free = dict.fromkeys(STEP, 0.0)
    arrived, order = {}, []
    left = set(pieces)
    while left:
        best = None
        for x in left:
            kids = CHILDREN.get(x, [])
            if any(c not in arrived for _, c in kids):
                continue
            ready = max([arrived[c] for _, c in kids], default=0.0 if x[0][0] == first else 1.0)
            d = BACK[PARENT[x]]
            key = (max(free[d], ready), x[0][0] != first, -hops(x), PARTS.index(x[0]), x[1], x[2])
            if best is None or key < best[0]:
                best = (key, x, d)
        key, x, d = best
        left.remove(x)
        free[d] = key[0] + 1
        arrived[x] = key[0] + 1 + LATENCY
        order.append((x, key[0]))
    ends = {}
    for part in PARTS:
        ends[part] = max(arrived[c] for _, c in CHILDREN[part, 0, 0])
    return order, ends


GATHER = [x for x, _ in gather_order()]
SCATTER = [x for x, _ in scatter_order(1)[0]]
INDEX = {x: i for i, x in enumerate(GATHER)}
PLANES = {x: needed_planes(x) for x in GATHER}
NPIECE = len(GATHER)


def level(z, y, oz, oy):
    return lax.rem(z + oz + NZ, NZ) * NY + lax.rem(y + oy + NY, NY)


def toward(z, y, d):
    return {"depth": level(z, y, *STEP[d])}


def among(z, planes):
    if len(planes) == NZ:
        return None
    return functools.reduce(jnp.logical_or, [z == p for p in sorted(planes)]) if planes else False


def guarded(cond, fn):
    if cond is None:
        fn()
    elif cond is not False:
        pl.when(cond)(fn)


def shifted(planes, d):
    return frozenset((p - STEP[d][0]) % NZ for p in planes)


def half(ref, lev, part):
    rows = ref.shape[1] // HALVES
    return ref.at[lev, pl.ds(part[1] * rows, rows)]


def copy_to(src, dst, send_sem, recv_sem, i, dev):
    return pltpu.make_async_remote_copy(src_ref=src, dst_ref=dst, send_sem=send_sem.at[i], recv_sem=recv_sem.at[i], device_id=dev, device_id_type=MESH)


def gather_piece(z, y, x, bufs, sems):
    part, oz, oy = x
    ref = half(bufs[part[0]], level(z, y, oz, oy), part)
    return copy_to(ref, ref, *sems, INDEX[x], toward(z, y, "z+"))


def gather_sends(z, y, x, bufs, sems, go):
    part, oz, oy = x
    for d, c in CHILDREN.get(x, []):
        ref = half(bufs[part[0]], level(z, y, oz, oy), part)
        cp = copy_to(ref, ref, *sems, INDEX[c], toward(z, y, d))
        guarded(among(z, shifted(PLANES[c], d)), cp.start if go else cp.wait_send)


def gather_own(z, y, bufs, sems):
    for part in PARTS:
        gather_sends(z, y, (part, 0, 0), bufs, sems, True)


def gather_rest(z, y, bufs, sems):
    for x in GATHER:
        def step(x=x):
            gather_piece(z, y, x, bufs, sems).wait_recv()
            gather_sends(z, y, x, bufs, sems, True)
        guarded(among(z, PLANES[x]), step)


def gather_drain(z, y, bufs, sems):
    for part in PARTS:
        gather_sends(z, y, (part, 0, 0), bufs, sems, False)
    for x in GATHER:
        gather_sends(z, y, x, bufs, sems, False)


def leaf_planes(x):
    out = set(PLANES[x])
    for d, c in CHILDREN.get(x, []):
        out -= shifted(PLANES[c], d)
    return frozenset(out)


def scatter_send(z, y, x, bufs, land, sems):
    part, oz, oy = x
    return copy_to(half(bufs[part[0]], level(z, y, oz, oy), part), land.at[INDEX[x]], *sems, INDEX[x], toward(z, y, BACK[PARENT[x]]))


def scatter_leaves(z, y, tensor, bufs, land, sems):
    for x in SCATTER:
        if x[0][0] == tensor:
            guarded(among(z, leaf_planes(x)), lambda x=x: scatter_send(z, y, x, bufs, land, sems).start())


def scatter_total(z, y, x, bufs, land, sems):
    part, oz, oy = x
    total = half(bufs[part[0]], level(z, y, oz, oy), part)
    kids = [c for d, c in CHILDREN.get(x, [])]
    for d, c in CHILDREN.get(x, []):
        i = INDEX[c]
        arrival = copy_to(land.at[i], land.at[i], *sems, i, toward(z, y, "z+"))
        guarded(among(z, shifted(PLANES[c], d)), arrival.wait_recv)
    total = total[...].astype(f32)
    for c in kids:
        total = total + land[INDEX[c]].astype(f32)
    return total


def scatter_inner(z, y, x, bufs, land, sems):
    part, oz, oy = x
    def step():
        half(bufs[part[0]], level(z, y, oz, oy), part)[...] = scatter_total(z, y, x, bufs, land, sems).astype(bf16)
        scatter_send(z, y, x, bufs, land, sems).start()
    guarded(among(z, PLANES[x] - leaf_planes(x)), step)


def scatter_own(z, y, tensor, bufs, land, sems):
    return jnp.concatenate([scatter_total(z, y, (part, 0, 0), bufs, land, sems) for part in PARTS if part[0] == tensor], axis=0)


def scatter_drain(z, y, bufs, land, sems):
    for x in SCATTER:
        guarded(among(z, PLANES[x]), lambda x=x: scatter_send(z, y, x, bufs, land, sems).wait_send())


def spread(buf, mine, sems, base, n, device, part):
    buf[mine] = part
    copies = []
    for j in range(1, n):
        cp = copy_to(buf.at[mine], buf.at[mine], *sems, base + j - 1, device(j))
        cp.start()
        copies.append(cp)
    return copies


def collect(buf, n, copies):
    for cp in copies:
        cp.wait_recv()
    total = buf[0]
    for j in range(1, n):
        total = total + buf[j]
    return total


def greet(z, y, h, nh):
    peers = [{"heads": lax.rem(h + j, nh)} for j in range(1, nh)]
    peers += [{"depth": level(z, y, j, 0)} for j in range(1, NZ)]
    peers += [{"depth": level(z, y, 0, j)} for j in range(1, NY)]
    bar = pltpu.get_barrier_semaphore()
    for d in peers:
        pl.semaphore_signal(bar, inc=1, device_id=d, device_id_type=MESH)
    return lambda: pl.semaphore_wait(bar, len(peers))

LEVELS = NZ * NY
HEADS = 8
R = HEADS * BLOCK
KT = LEVELS * BLOCK


def dot(a, b):
    return jnp.dot(a, b, preferred_element_type=f32)


def dot_lhs_t(a, b):
    return lax.dot_general(a, b, (((0,), (0,)), ((), ())), preferred_element_type=f32)


def normed(rows):
    x = rows.astype(f32)
    inv = 1.0 / jnp.sqrt(jnp.mean(x * x, axis=-1, keepdims=True) + EPS)
    return x * inv, inv


def norm_backward(grad, hat, inv, gain):
    gh = grad * gain
    return inv * (gh - hat * jnp.mean(gh * hat, axis=-1, keepdims=True))


def fused_kernel(nh, LC, RT, mask_ref, count_ref, q_ref, g_ref, k_ref, v_ref, qg_ref, kg_ref,
                 out_ref, gq_ref, gk_ref, gv_ref, gain_ref,
                 ka, va, kx, vx, s_scr, qT, gT, qrows, grows, ot, dqt, dk, dv, ml, pk, pv, land, o_scr, gq_scr,
                 arh, arz, ary, gsend, grecv, ssend, srecv, asend, arecv, lsem):
    pos = lax.axis_index("depth")
    h = lax.axis_index("heads")
    z, y = pos // NY, pos % NY
    gsem, ssem, asem = (gsend, grecv), (ssend, srecv), (asend, arecv)
    kv, parts = (ka, va), (pk, pv)
    greeted = greet(z, y, h, nh)
    k_hat, k_inv = normed(k_ref[...])
    ka[pos] = (k_hat * kg_ref[...]).astype(bf16)
    va[pos] = v_ref[...]
    land[...] = jnp.zeros_like(land)
    greeted()
    gather_own(z, y, kv, gsem)

    nl = pos + 1
    nch = (nl + LC - 1) // LC
    CK = LC * BLOCK
    NRT = R // RT
    gain = qg_ref[...]
    lane = lax.broadcasted_iota(jnp.int32, (BLOCK, BLOCK), 1)
    sub = lax.broadcasted_iota(jnp.int32, (BLOCK, BLOCK), 0)
    causal = jnp.where(sub <= lane, 0.0, NEG).astype(f32)
    causal = jnp.concatenate([causal] * (RT // BLOCK), axis=1)
    extra = lax.broadcasted_iota(jnp.int32, (BLOCK, R), 0)

    def prepare(b):
        rows = pl.ds(b * BLOCK, BLOCK)
        qT[b, 128:256, :] = jnp.where(extra == 0, 1.0, 0.0).astype(bf16)
        for i in range(HEADS):
            hs = slice(i * 128, (i + 1) * 128)
            hat, inv = normed(q_ref[rows, hs])
            low = (hat * gain).astype(bf16)
            qrows[b, hs, :] = low
            qT[b, 0:128, hs] = low.T
            gr = g_ref[rows, hs]
            grows[b, hs, :] = gr
            gT[b, 0:128, hs] = gr.T

    for b in range(2):
        prepare(b)

    def fill(i, _):
        pk[i] = jnp.zeros((2 * BLOCK, DH), bf16)
        pv[i] = jnp.zeros((2 * BLOCK, DH), bf16)
        return 0

    lax.fori_loop(nl, LEVELS, fill, 0)
    gather_rest(z, y, kv, gsem)

    def chunk(c):
        return pl.ds(pl.multiple_of(c * CK, CK), CK)

    def combine(src, dst):
        def one(i, _):
            ks = pl.ds(pl.multiple_of((i + 1) * BLOCK, BLOCK), BLOCK)
            m0 = mask_ref[2 * pos, 2 * i + 1]
            m1 = mask_ref[2 * pos + 1, 2 * i + 1]
            a0 = src[0, ks, :]
            a1 = src[1, ks, :]
            for m in range(2):
                both = jnp.where(m0 == m, a0, 0.0) + jnp.where(m1 == m, a1, 0.0)
                dst[i, m * BLOCK:(m + 1) * BLOCK, :] = both.astype(bf16)
            return 0

        lax.fori_loop(0, pos, one, 0)
        for b in range(2):
            dst[pos, b * BLOCK:(b + 1) * BLOCK, :] = src[b, 0:BLOCK, :].astype(bf16)

    q_part = jnp.zeros((1, DH), f32)
    ml[3:4, 0:DH] = jnp.zeros((1, DH), f32)
    for b in range(2):
        own = 2 * pos + b

        def gather(s, _):
            first = s == 0
            lev = jnp.where(first, pos, jnp.minimum(s - 1, pos))
            m = jnp.where(first, b, mask_ref[own, 2 * lev + 1])
            cnt = jnp.where(m == 1, count_ref[2 * lev + 1], count_ref[2 * lev])
            cnt = jnp.where(s < nl, cnt, 0)
            ks = pl.ds(pl.multiple_of(s * BLOCK, BLOCK), BLOCK)
            kx[ks, 0:128] = jnp.where(m == 1, ka[lev, 128:256], ka[lev, 0:128])
            vx[ks, 0:128] = jnp.where(m == 1, va[lev, 128:256], va[lev, 0:128])
            bias = jnp.where(sub < cnt, 0.0, NEG)
            kx[ks, 128:256] = jnp.where(lane == 0, bias, 0.0).astype(bf16)
            vx[ks, 128:256] = jnp.where(lane < 3, -1.0, 0.0).astype(bf16)
            return 0

        lax.fori_loop(0, nch * LC, gather, 0)
        ml[0:1, :] = jnp.full((1, R), NEG, f32)
        ml[1:2, :] = jnp.zeros((1, R), f32)

        def pass1(c, first):
            ks = chunk(c)
            kc = kx[ks, :]
            for r in range(NRT):
                rs = slice(r * RT, (r + 1) * RT)
                s = dot(kc, qT[b, :, rs])
                if first:
                    s = jnp.concatenate([s[0:BLOCK] + causal, s[BLOCK:]], axis=0)
                s_scr[ks, rs] = s
                old = ml[0:1, rs]
                new = jnp.maximum(old, jnp.max(s, axis=0, keepdims=True))
                e = jnp.exp2((s - new) * C2)
                ml[1:2, rs] = ml[1:2, rs] * jnp.exp2((old - new) * C2) + jnp.sum(e, axis=0, keepdims=True)
                ml[0:1, rs] = new

        pass1(0, True)

        def later(c, _):
            pass1(c, False)
            return 0

        lax.fori_loop(1, nch, later, 0)
        ml[2:3, :] = ml[0:1, :] * C2 + jnp.log2(ml[1:2, :])
        ot[...] = jnp.zeros_like(ot)
        dqt[...] = jnp.zeros_like(dqt)

        def forward(c, _):
            ks = chunk(c)
            vc = vx[ks, 0:128]
            acc = None
            for r in range(NRT):
                rs = slice(r * RT, (r + 1) * RT)
                p = jnp.exp2(s_scr[ks, rs] * C2 - ml[2:3, rs])
                s_scr[ks, rs] = p
                low = p.astype(bf16)
                ot[:, rs] += dot_lhs_t(vc, low)
                t = dot(low, grows[b, rs, :])
                acc = t if acc is None else acc + t
            dv[b, ks, :] = acc
            return 0

        lax.fori_loop(0, nch, forward, 0)
        if b == 1:
            combine(dv, pv)
            scatter_leaves(z, y, 1, parts, land, ssem)
        olow = ot[...].astype(bf16)
        delta = jnp.sum(olow.astype(f32) * gT[b, 0:128, :].astype(f32), axis=0, keepdims=True)
        d0 = delta.astype(bf16)
        r1 = delta - d0.astype(f32)
        d1 = r1.astype(bf16)
        d2 = (r1 - d1.astype(f32)).astype(bf16)
        pieces = jnp.where(extra == 0, d0.astype(f32), jnp.where(extra == 1, d1.astype(f32), jnp.where(extra == 2, d2.astype(f32), 0.0)))
        gT[b, 128:256, :] = pieces.astype(bf16)
        rows = pl.ds(b * BLOCK, BLOCK)
        for i in range(HEADS):
            hs = slice(i * 128, (i + 1) * 128)
            o_scr[rows, hs] = olow[:, hs].T

        def backward(c, _):
            ks = chunk(c)
            vc = vx[ks, :]
            kc = kx[ks, 0:128]
            acc = None
            for r in range(NRT):
                rs = slice(r * RT, (r + 1) * RT)
                dp = dot(vc, gT[b, :, rs])
                ds = (s_scr[ks, rs] * dp).astype(bf16)
                dqt[:, rs] += dot_lhs_t(kc, ds)
                t = dot(ds, qrows[b, rs, :])
                acc = t if acc is None else acc + t
            acc = acc * SCALE
            dk[b, ks, :] = acc
            ml[3:4, 0:DH] += jnp.sum(acc * kc.astype(f32), axis=0, keepdims=True)
            return 0

        lax.fori_loop(0, nch, backward, 0)
        if b == 1:
            combine(dk, pk)
            scatter_leaves(z, y, 0, parts, land, ssem)
        for i in range(HEADS):
            hs = slice(i * 128, (i + 1) * 128)
            gqn = dqt[:, hs].T * SCALE
            hat, inv = normed(q_ref[rows, hs])
            gq_scr[rows, hs] = norm_backward(gqn, hat, inv, gain).astype(bf16)
            q_part = q_part + jnp.sum(gqn * hat, axis=0, keepdims=True)
    done = [pltpu.make_async_copy(o_scr, out_ref, lsem.at[0]), pltpu.make_async_copy(gq_scr, gq_ref, lsem.at[1])]
    for cp in done:
        cp.start()
    gains = jnp.concatenate([q_part, ml[3:4, 0:DH] / kg_ref[...], jnp.zeros((6, DH), f32)], axis=0)
    c1 = spread(arh, h, asem, 0, nh, lambda j: {"heads": lax.rem(h + j, nh)}, gains)
    inner_v = [x for x in SCATTER if x[0][0] == 1]
    inner_k = [x for x in SCATTER if x[0][0] == 0]
    for x in inner_v:
        scatter_inner(z, y, x, parts, land, ssem)
    c2 = spread(arz, z, asem, nh - 1, NZ, lambda j: {"depth": level(z, y, j, 0)}, collect(arh, nh, c1))
    for x in inner_k[:len(inner_k) // 2]:
        scatter_inner(z, y, x, parts, land, ssem)
    c3 = spread(ary, y, asem, nh + NZ - 2, NY, lambda j: {"depth": level(z, y, 0, j)}, collect(arz, NZ, c2))
    for x in inner_k[len(inner_k) // 2:]:
        scatter_inner(z, y, x, parts, land, ssem)
    gv_ref[...] = scatter_own(z, y, 1, parts, land, ssem).astype(bf16)
    k_hat, k_inv = normed(k_ref[...])
    gk_ref[...] = norm_backward(scatter_own(z, y, 0, parts, land, ssem), k_hat, k_inv, kg_ref[...]).astype(bf16)
    gain_ref[...] = collect(ary, NY, c3)
    for cp in c1 + c2 + c3:
        cp.wait_send()
    gather_drain(z, y, kv, gsem)
    scatter_drain(z, y, parts, land, ssem)
    for cp in done:
        cp.wait()


def fused(mask, count, q, g, k, v, qg, kg, nh, LC=16, RT=256):
    vmem = pl.BlockSpec(memory_space=pltpu.VMEM)
    smem = pl.BlockSpec(memory_space=pltpu.SMEM)
    hbm = pl.BlockSpec(memory_space=pl.ANY)
    sd = jax.ShapeDtypeStruct
    na = nh + NZ + NY - 3
    rows = k.shape[0]
    V = pltpu.VMEM
    dma = pltpu.SemaphoreType.DMA
    return pl.pallas_call(
        functools.partial(fused_kernel, nh, LC, RT),
        out_shape=(sd(q.shape, bf16), sd(q.shape, bf16), sd(k.shape, bf16), sd(k.shape, bf16), sd((8, DH), f32)),
        in_specs=[smem, smem] + [vmem] * 6,
        out_specs=(hbm, hbm, vmem, vmem, vmem),
        scratch_shapes=[
            V((LEVELS, rows, DH), bf16), V((LEVELS, rows, DH), bf16), V((KT, 256), bf16), V((KT, 256), bf16), V((KT, R), f32),
            V((2, 256, R), bf16), V((2, 256, R), bf16), V((2, R, DH), bf16), V((2, R, DH), bf16),
            V((DH, R), f32), V((DH, R), f32), V((2, KT, DH), f32), V((2, KT, DH), f32), V((8, R), f32),
            V((LEVELS, rows, DH), bf16), V((LEVELS, rows, DH), bf16), V((NPIECE, rows // HALVES, DH), bf16),
            V(q.shape, bf16), V(q.shape, bf16),
            V((nh, 8, DH), f32), V((NZ, 8, DH), f32), V((NY, 8, DH), f32),
        ] + [dma((NPIECE,))] * 4 + [dma((na,))] * 2 + [dma((2,))],
        compiler_params=pltpu.CompilerParams(collective_id=0, has_side_effects=True, vmem_limit_bytes=60 * 2**20),
        name="tree_attention",
    )(mask, count, q, g, k, v, qg, kg)


def hand_on_kernel(*refs):
    n = len(refs) // 2
    for i in range(n):
        refs[n + i][...] = refs[i][...]


def hand_on(arrays):
    vmem = pl.BlockSpec(memory_space=pltpu.VMEM)
    n = len(arrays)
    return pl.pallas_call(
        hand_on_kernel,
        out_shape=tuple(jax.ShapeDtypeStruct(a.shape, a.dtype) for a in arrays),
        in_specs=[vmem] * n,
        out_specs=(vmem,) * n,
        name="hand_on",
    )(*arrays)


def body(q_raw, k_raw, values, q_gain, k_gain, grad_out, block_mask, block_count):
    out, gq, gk, gv, gains = fused(
        block_mask, block_count, q_raw, grad_out, k_raw, values,
        q_gain.reshape(1, DH), k_gain.reshape(1, DH), lax.axis_size("heads"),
    )
    out, gq, gk, gv, gains = hand_on((out, gq, gk, gv, gains))
    return out, gq, gk, gv, gains[0], gains[1]


def solution(mesh):
    rows = P("depth", "heads")
    return jax.shard_map(
        body,
        mesh=mesh,
        in_specs=(rows, rows, rows, P(), P(), rows, P(), P()),
        out_specs=(rows, rows, rows, rows, P(), P()),
        check_vma=False,
    )
```

time: 955 us -> 123 us (0.13)
  waiting for transfers between devices: 747 us -> 0 us
  Pallas kernels: 0 us -> 121 us
  blocking collectives: 73.5 us -> 0 us
  local copies, waits for them, and re-layouts: 63.3 us -> 1.28 us
  other arithmetic: 30.6 us -> 0 us
  between operations: 13.8 us -> 0.64 us
  loops' own time: 12.7 us -> 0 us
    reduce_scatter x1 -> x0, waiting for transfers between devices: 596 us -> none  [body(): lax.psum_scatter(partial_value.reshape(nblocks * BLOCK, kv_local * 2 * DH...]
    all_gather x2 -> x0, waiting for transfers between devices: 150 us -> none  [the longest x1 76.7 us: body(): lax.all_gather(values.reshape(row_count, kv_local, DH), 'depth', axis=0,...]
    pallas_call x0 -> x2, Pallas kernels: none -> 121 us  [the longest x1 119 us: fused(): pl.pallas_call(functools.partial(fused_kernel, nh, LC, RT), out_shape=(sd...]
    psum x1 -> x0, blocking collectives: 73.5 us -> none  [body(): lax.psum((q_gain_part, k_gain_part), ('depth', 'heads'))]
    gather x16 -> x0, local copies, waits for them, and re-layouts: 19.1 us -> none  [the longest x4 8.65 us: score_tile(): tile_values = values_all[picked].reshape(LEVEL_GROUP * BLOCK, kv_local, DH)]
    dynamic_update_slice x8 -> x0, other arithmetic: 12.8 us -> none  [backward(): lax.dynamic_update_slice_in_dim(partial_now, current + pieces[level_slot]...]
    another operation x7 -> x0, loops' own time: 12.7 us -> none  [the longest x1 6.9 us: body(): lax.scan(attend, (start_partial, start_gain), (work_q, work_g, work_ids))]
    while x19 -> x0, local copies, waits for them, and re-layouts: 12.5 us -> none  [the longest x1 7.24 us: body(): lax.scan(attend, (start_partial, start_gain), (work_q, work_g, work_ids))]
  transfers between devices with their start and end apart: 3 -> 0, of which waited for: 3 -> 0; matrix products, arithmetic and copies ran while one was open for 1% -> 0% of each run, Pallas kernels for 0% -> 0%
where the time goes in v2:
time: 123 us
  Pallas kernels  121 us (98%)
  local copies, waits for them, and re-layouts  1.28 us (1%)
    pallas_call x1, Pallas kernels, fused(): pl.pallas_call(functools.partial(fused_kernel, nh, LC, RT), out_shape=(sd...  119 us

profile of v2, /device:TPU:2, one launch (start us, length us, event | category | flops | bytes accessed | tf_op | source)
XLA Modules:
  0.0 122.8 jit_solution(9554482380365538837)
XLA Ops:
  0.6 118.6 %tree_attention.1 = (bf16[256,1024]{1,0:T(8,128)(2,1)}, bf16[256,1024]{1,0:T(8,128)(2,1)}, bf16[256,128]{1,0:T(8,128)(2,1)}, bf16[256,128]{1,0:T(8,128)(2,1)}, f32[8,128]{1,0:T(8,128)}) custom-call(s32[64,64]{1,0:T(8,128)} %mask_ref.1, s32[64]{0:T(128)} %count_ref.1, bf16[256,1024]{1,0:T(8,128)(2,1)} %q_ref.1, bf16[256,1024]{1,0:T(8,128)(2,1)} %g_ref.1, ...), custom_call_target="tpu_custom_call" | custom-call | tf_op jit(solution)/shard_map/tree_attention/pallas_call | solution.py:527
  119.2 2.3 %hand_on.1 = (bf16[256,1024]{1,0:T(8,128)(2,1)}, bf16[256,1024]{1,0:T(8,128)(2,1)}, bf16[256,128]{1,0:T(8,128)(2,1)}, bf16[256,128]{1,0:T(8,128)(2,1)}, f32[8,128]{1,0:T(8,128)}) custom-call(bf16[256,1024]{1,0:T(8,128)(2,1)} %get-tuple-element.16.refs_0_, bf16[256,1024]{1,0:T(8,128)(2,1)} %get-tuple-element.17.refs_1_, ...), custom_call_target="tpu_custom_call" | custom-call | tf_op jit(solution)/shard_map/hand_on/pallas_call | solution.py:554
  121.5 1.3 %slice_bitcast_fusion = (f32[128]{0:T(128)}, f32[128]{0:T(128)}) fusion(f32[8,128]{1,0:T(8,128)} %get-tuple-element.25), kind=kLoop, calls=%fused_computation | loop fusion | bytes 2048 | tf_op jit(solution)/shard_map/squeeze | solution.py:569

commit v3 on v2

--- a/solution.py
+++ b/solution.py
@@ -90,7 +90,7 @@
     def push(x, at):
         nonlocal count
         for d, c in CHILDREN.get(x, []):
-            waiting.append((at, (x[0][0], -height(c), count), d, c))
+            waiting.append((at, (-height(c), count), d, c))
             count += 1
     for part in PARTS:
         push((part, 0, 0), 0.0)
@@ -105,35 +105,31 @@
     return [(c, t) for t, _, c in done]
 
 
-def scatter_order(first):
-    pieces = list(PARENT)
-    free = dict.fromkeys(STEP, 0.0)
+def scatter_order(lead):
+    free = dict.fromkeys(STEP, -lead)
     arrived, order = {}, []
-    left = set(pieces)
+    left = set(PARENT)
     while left:
         best = None
         for x in left:
             kids = CHILDREN.get(x, [])
             if any(c not in arrived for _, c in kids):
                 continue
-            ready = max([arrived[c] for _, c in kids], default=0.0 if x[0][0] == first else 1.0)
+            ready = max([arrived[c] for _, c in kids], default=-lead if x[0][0] == 1 else 0.0)
             d = BACK[PARENT[x]]
-            key = (max(free[d], ready), x[0][0] != first, -hops(x), PARTS.index(x[0]), x[1], x[2])
+            key = (max(free[d], ready), -hops(x), PARTS.index(x[0]), x[1], x[2])
             if best is None or key < best[0]:
                 best = (key, x, d)
         key, x, d = best
         left.remove(x)
         free[d] = key[0] + 1
         arrived[x] = key[0] + 1 + LATENCY
-        order.append((x, key[0]))
-    ends = {}
-    for part in PARTS:
-        ends[part] = max(arrived[c] for _, c in CHILDREN[part, 0, 0])
-    return order, ends
+        order.append(x)
+    return order
 
 
 GATHER = [x for x, _ in gather_order()]
-SCATTER = [x for x, _ in scatter_order(1)[0]]
+SCATTER = scatter_order(0.0)
 INDEX = {x: i for i, x in enumerate(GATHER)}
 PLANES = {x: needed_planes(x) for x in GATHER}
 NPIECE = len(GATHER)
@@ -192,8 +188,8 @@
         gather_sends(z, y, (part, 0, 0), bufs, sems, True)
 
 
-def gather_rest(z, y, bufs, sems):
-    for x in GATHER:
+def gather_rest(z, y, bufs, sems, pieces):
+    for x in pieces:
         def step(x=x):
             gather_piece(z, y, x, bufs, sems).wait_recv()
             gather_sends(z, y, x, bufs, sems, True)
@@ -219,10 +215,15 @@
     return copy_to(half(bufs[part[0]], level(z, y, oz, oy), part), land.at[INDEX[x]], *sems, INDEX[x], toward(z, y, BACK[PARENT[x]]))
 
 
-def scatter_leaves(z, y, tensor, bufs, land, sems):
+def scatter_leaves(z, y, tensor, bufs, land, sems, chosen=None):
     for x in SCATTER:
-        if x[0][0] == tensor:
-            guarded(among(z, leaf_planes(x)), lambda x=x: scatter_send(z, y, x, bufs, land, sems).start())
+        planes = leaf_planes(x)
+        if planes and x[0][0] == tensor:
+            cond = among(z, planes)
+            if chosen is not None:
+                pick = chosen(level(z, y, x[1], x[2]))
+                cond = pick if cond is None else jnp.logical_and(cond, pick)
+            guarded(cond, lambda x=x: scatter_send(z, y, x, bufs, land, sems).start())
 
 
 def scatter_total(z, y, x, bufs, land, sems):
@@ -310,7 +311,7 @@
 
 
 def fused_kernel(nh, LC, RT, mask_ref, count_ref, q_ref, g_ref, k_ref, v_ref, qg_ref, kg_ref,
-                 out_ref, gq_ref, gk_ref, gv_ref, gain_ref,
+                 out_ref, gq_ref, gk_ref, gv_ref, qgain_ref, kgain_ref,
                  ka, va, kx, vx, s_scr, qT, gT, qrows, grows, ot, dqt, dk, dv, ml, pk, pv, land, o_scr, gq_scr,
                  arh, arz, ary, gsend, grecv, ssend, srecv, asend, arecv, lsem):
     pos = lax.axis_index("depth")
@@ -350,42 +351,54 @@
             grows[b, hs, :] = gr
             gT[b, 0:128, hs] = gr.T
 
-    for b in range(2):
-        prepare(b)
+    prepare(0)
 
     def fill(i, _):
         pk[i] = jnp.zeros((2 * BLOCK, DH), bf16)
         pv[i] = jnp.zeros((2 * BLOCK, DH), bf16)
         return 0
 
-    lax.fori_loop(nl, LEVELS, fill, 0)
-    gather_rest(z, y, kv, gsem)
+    lax.fori_loop(NY * (z + 1), LEVELS, fill, 0)
+    gather_rest(z, y, kv, gsem, GATHER[:NPIECE // 3])
+    prepare(1)
+    gather_rest(z, y, kv, gsem, GATHER[NPIECE // 3:])
+
+    def tile(c, t):
+        size = NY * BLOCK
+        return pl.ds(pl.multiple_of(c * CK + t * size, size), size)
 
     def chunk(c):
         return pl.ds(pl.multiple_of(c * CK, CK), CK)
 
-    def combine(src, dst):
-        def one(i, _):
-            ks = pl.ds(pl.multiple_of((i + 1) * BLOCK, BLOCK), BLOCK)
+    def combine(src, dst, start, stop):
+        def one(i):
+            ks = pl.ds(pl.multiple_of(jnp.minimum(i + 1, LEVELS - 1) * BLOCK, BLOCK), BLOCK)
             m0 = mask_ref[2 * pos, 2 * i + 1]
             m1 = mask_ref[2 * pos + 1, 2 * i + 1]
-            a0 = src[0, ks, :]
-            a1 = src[1, ks, :]
+            a0 = jnp.where(i < pos, src[0, ks, :], 0.0)
+            a1 = jnp.where(i < pos, src[1, ks, :], 0.0)
             for m in range(2):
                 both = jnp.where(m0 == m, a0, 0.0) + jnp.where(m1 == m, a1, 0.0)
                 dst[i, m * BLOCK:(m + 1) * BLOCK, :] = both.astype(bf16)
+
+        def four(i, _):
+            for t in range(4):
+                one(4 * i + t)
             return 0
 
-        lax.fori_loop(0, pos, one, 0)
-        for b in range(2):
-            dst[pos, b * BLOCK:(b + 1) * BLOCK, :] = src[b, 0:BLOCK, :].astype(bf16)
+        lax.fori_loop(jnp.maximum(start, 0), stop, four, 0)
+        def own_level():
+            for b in range(2):
+                dst[pos, b * BLOCK:(b + 1) * BLOCK, :] = src[b, 0:BLOCK, :].astype(bf16)
+
+        pl.when(stop == z + 1)(own_level)
 
     q_part = jnp.zeros((1, DH), f32)
     ml[3:4, 0:DH] = jnp.zeros((1, DH), f32)
     for b in range(2):
         own = 2 * pos + b
 
-        def gather(s, _):
+        def gather_slot(s):
             first = s == 0
             lev = jnp.where(first, pos, jnp.minimum(s - 1, pos))
             m = jnp.where(first, b, mask_ref[own, 2 * lev + 1])
@@ -396,10 +409,15 @@
             vx[ks, 0:128] = jnp.where(m == 1, va[lev, 128:256], va[lev, 0:128])
             bias = jnp.where(sub < cnt, 0.0, NEG)
             kx[ks, 128:256] = jnp.where(lane == 0, bias, 0.0).astype(bf16)
-            vx[ks, 128:256] = jnp.where(lane < 3, -1.0, 0.0).astype(bf16)
+            if b == 0:
+                vx[ks, 128:256] = jnp.where(lane < 3, -1.0, 0.0).astype(bf16)
+
+        def gather(i, _):
+            for t in range(4):
+                gather_slot(4 * i + t)
             return 0
 
-        lax.fori_loop(0, nch * LC, gather, 0)
+        lax.fori_loop(0, nch * (LC // 4), gather, 0)
         ml[0:1, :] = jnp.full((1, R), NEG, f32)
         ml[1:2, :] = jnp.zeros((1, R), f32)
 
@@ -430,23 +448,18 @@
         dqt[...] = jnp.zeros_like(dqt)
 
         def forward(c, _):
-            ks = chunk(c)
-            vc = vx[ks, 0:128]
-            acc = None
-            for r in range(NRT):
-                rs = slice(r * RT, (r + 1) * RT)
-                p = jnp.exp2(s_scr[ks, rs] * C2 - ml[2:3, rs])
-                s_scr[ks, rs] = p
+            for t in range(LC // NY):
+                ks = tile(c, t)
+                p = jnp.exp2(s_scr[ks, :] * C2 - ml[2:3, :])
+                s_scr[ks, :] = p
                 low = p.astype(bf16)
-                ot[:, rs] += dot_lhs_t(vc, low)
-                t = dot(low, grows[b, rs, :])
-                acc = t if acc is None else acc + t
-            dv[b, ks, :] = acc
+                ot[...] += dot_lhs_t(vx[ks, 0:128], low)
+                dv[b, ks, :] = dot(low, grows[b])
             return 0
 
         lax.fori_loop(0, nch, forward, 0)
         if b == 1:
-            combine(dv, pv)
+            combine(dv, pv, 0, z + 1)
             scatter_leaves(z, y, 1, parts, land, ssem)
         olow = ot[...].astype(bf16)
         delta = jnp.sum(olow.astype(f32) * gT[b, 0:128, :].astype(f32), axis=0, keepdims=True)
@@ -462,26 +475,27 @@
             o_scr[rows, hs] = olow[:, hs].T
 
         def backward(c, _):
-            ks = chunk(c)
-            vc = vx[ks, :]
-            kc = kx[ks, 0:128]
-            acc = None
-            for r in range(NRT):
-                rs = slice(r * RT, (r + 1) * RT)
-                dp = dot(vc, gT[b, :, rs])
-                ds = (s_scr[ks, rs] * dp).astype(bf16)
-                dqt[:, rs] += dot_lhs_t(kc, ds)
-                t = dot(ds, qrows[b, rs, :])
-                acc = t if acc is None else acc + t
-            acc = acc * SCALE
-            dk[b, ks, :] = acc
-            ml[3:4, 0:DH] += jnp.sum(acc * kc.astype(f32), axis=0, keepdims=True)
+            for t in range(LC // NY):
+                ks = tile(c, t)
+                kc = kx[ks, 0:128]
+                dp = dot(vx[ks, :], gT[b])
+                ds = (s_scr[ks, :] * dp).astype(bf16)
+                dqt[...] += dot_lhs_t(kc, ds)
+                acc = dot(ds, qrows[b]) * SCALE
+                dk[b, ks, :] = acc
+                ml[3:4, 0:DH] += jnp.sum(acc * kc.astype(f32), axis=0, keepdims=True)
             return 0
 
-        lax.fori_loop(0, nch, backward, 0)
-        if b == 1:
-            combine(dk, pk)
-            scatter_leaves(z, y, 0, parts, land, ssem)
+        if b == 0:
+            lax.fori_loop(0, nch, backward, 0)
+        else:
+            early = (nch - 1) * (LC // NY - 1)
+            lax.fori_loop(0, nch - 1, backward, 0)
+            combine(dk, pk, 0, early)
+            scatter_leaves(z, y, 0, parts, land, ssem, lambda lev: lev < NY * early)
+            lax.fori_loop(nch - 1, nch, backward, 0)
+            combine(dk, pk, early, z + 1)
+            scatter_leaves(z, y, 0, parts, land, ssem, lambda lev: lev >= NY * early)
         for i in range(HEADS):
             hs = slice(i * 128, (i + 1) * 128)
             gqn = dqt[:, hs].T * SCALE
@@ -493,20 +507,21 @@
         cp.start()
     gains = jnp.concatenate([q_part, ml[3:4, 0:DH] / kg_ref[...], jnp.zeros((6, DH), f32)], axis=0)
     c1 = spread(arh, h, asem, 0, nh, lambda j: {"heads": lax.rem(h + j, nh)}, gains)
-    inner_v = [x for x in SCATTER if x[0][0] == 1]
-    inner_k = [x for x in SCATTER if x[0][0] == 0]
-    for x in inner_v:
+    third = len(SCATTER) // 3
+    for x in SCATTER[:third]:
         scatter_inner(z, y, x, parts, land, ssem)
     c2 = spread(arz, z, asem, nh - 1, NZ, lambda j: {"depth": level(z, y, j, 0)}, collect(arh, nh, c1))
-    for x in inner_k[:len(inner_k) // 2]:
+    for x in SCATTER[third:2 * third]:
         scatter_inner(z, y, x, parts, land, ssem)
     c3 = spread(ary, y, asem, nh + NZ - 2, NY, lambda j: {"depth": level(z, y, 0, j)}, collect(arz, NZ, c2))
-    for x in inner_k[len(inner_k) // 2:]:
+    for x in SCATTER[2 * third:]:
         scatter_inner(z, y, x, parts, land, ssem)
     gv_ref[...] = scatter_own(z, y, 1, parts, land, ssem).astype(bf16)
     k_hat, k_inv = normed(k_ref[...])
     gk_ref[...] = norm_backward(scatter_own(z, y, 0, parts, land, ssem), k_hat, k_inv, kg_ref[...]).astype(bf16)
-    gain_ref[...] = collect(ary, NY, c3)
+    total = collect(ary, NY, c3)
+    qgain_ref[...] = total[0:1]
+    kgain_ref[...] = total[1:2]
     for cp in c1 + c2 + c3:
         cp.wait_send()
     gather_drain(z, y, kv, gsem)
@@ -526,9 +541,9 @@
     dma = pltpu.SemaphoreType.DMA
     return pl.pallas_call(
         functools.partial(fused_kernel, nh, LC, RT),
-        out_shape=(sd(q.shape, bf16), sd(q.shape, bf16), sd(k.shape, bf16), sd(k.shape, bf16), sd((8, DH), f32)),
+        out_shape=(sd(q.shape, bf16), sd(q.shape, bf16), sd(k.shape, bf16), sd(k.shape, bf16), sd((1, DH), f32), sd((1, DH), f32)),
         in_specs=[smem, smem] + [vmem] * 6,
-        out_specs=(hbm, hbm, vmem, vmem, vmem),
+        out_specs=(hbm, hbm, vmem, vmem, vmem, vmem),
         scratch_shapes=[
             V((LEVELS, rows, DH), bf16), V((LEVELS, rows, DH), bf16), V((KT, 256), bf16), V((KT, 256), bf16), V((KT, R), f32),
             V((2, 256, R), bf16), V((2, 256, R), bf16), V((2, R, DH), bf16), V((2, R, DH), bf16),
@@ -561,12 +576,12 @@
 
 
 def body(q_raw, k_raw, values, q_gain, k_gain, grad_out, block_mask, block_count):
-    out, gq, gk, gv, gains = fused(
+    results = fused(
         block_mask, block_count, q_raw, grad_out, k_raw, values,
         q_gain.reshape(1, DH), k_gain.reshape(1, DH), lax.axis_size("heads"),
     )
-    out, gq, gk, gv, gains = hand_on((out, gq, gk, gv, gains))
-    return out, gq, gk, gv, gains[0], gains[1]
+    out, gq, gk, gv, q_part, k_part = hand_on(results)
+    return out, gq, gk, gv, q_part.reshape(DH), k_part.reshape(DH)
 
 
 def solution(mesh):

time: 123 us -> 105 us (0.85)
  Pallas kernels: 121 us -> 104 us
  local copies, waits for them, and re-layouts: 1.28 us -> 0 us
    pallas_call x1, Pallas kernels: 119 us -> 102 us  [fused(): pl.pallas_call(functools.partial(fused_kernel, nh, LC, RT), out_shape=(sd...]
    squeeze x1 -> x0, local copies, waits for them, and re-layouts: 1.28 us -> none  [body(): return (out, gq, gk, gv, gains[0], gains[1])]
where the time goes in v3:
time: 105 us
  Pallas kernels  104 us (99%)
    pallas_call x1, Pallas kernels, fused(): pl.pallas_call(functools.partial(fused_kernel, nh, LC, RT), out_shape=(sd...  102 us
    pallas_call x1, Pallas kernels, hand_on(): pl.pallas_call(hand_on_kernel, out_shape=tuple((jax.ShapeDtypeStruct(a.sh...  2.26 us

profile of v3, /device:TPU:2, one launch (start us, length us, event | category | flops | bytes accessed | tf_op | source)
XLA Modules:
  0.0 104.7 jit_solution(1945784491988307417)
XLA Ops:
  0.6 101.8 %tree_attention.1 = (bf16[256,1024]{1,0:T(8,128)(2,1)}, bf16[256,1024]{1,0:T(8,128)(2,1)}, bf16[256,128]{1,0:T(8,128)(2,1)}, bf16[256,128]{1,0:T(8,128)(2,1)}, f32[1,128]{1,0:T(1,128)}, /*index=5*/f32[1,128]{1,0:T(1,128)}) custom-call(s32[64,64]{1,0:T(8,128)} %mask_ref.1, s32[64]{0:T(128)} %count_ref.1, bf16[256,1024]{1,0:T(8,128)(2,1)} %q_ref.1, ...), custom_call_target="tpu_custom_call" | custom-call | tf_op jit(solution)/shard_map/tree_attention/pallas_call | solution.py:542
  102.4 2.3 %hand_on.1 = (bf16[256,1024]{1,0:T(8,128)(2,1)}, bf16[256,1024]{1,0:T(8,128)(2,1)}, bf16[256,128]{1,0:T(8,128)(2,1)}, bf16[256,128]{1,0:T(8,128)(2,1)}, f32[1,128]{1,0:T(1,128)}, /*index=5*/f32[1,128]{1,0:T(1,128)}) custom-call(bf16[256,1024]{1,0:T(8,128)(2,1)} %get-tuple-element.18.refs_0_, bf16[256,1024]{1,0:T(8,128)(2,1)} %get-tuple-element.19.refs_1_, ...), custom_call_target="tpu_custom_call" | custom-call | tf_op jit(solution)/shard_map/hand_on/pallas_call | solution.py:569

commit v4 on v3

--- a/solution.py
+++ b/solution.py
@@ -351,7 +351,6 @@
             grows[b, hs, :] = gr
             gT[b, 0:128, hs] = gr.T
 
-    prepare(0)
 
     def fill(i, _):
         pk[i] = jnp.zeros((2 * BLOCK, DH), bf16)
@@ -359,9 +358,11 @@
         return 0
 
     lax.fori_loop(NY * (z + 1), LEVELS, fill, 0)
-    gather_rest(z, y, kv, gsem, GATHER[:NPIECE // 3])
+    gather_rest(z, y, kv, gsem, GATHER[:NPIECE // 4])
+    prepare(0)
+    gather_rest(z, y, kv, gsem, GATHER[NPIECE // 4:NPIECE // 2])
     prepare(1)
-    gather_rest(z, y, kv, gsem, GATHER[NPIECE // 3:])
+    gather_rest(z, y, kv, gsem, GATHER[NPIECE // 2:])
 
     def tile(c, t):
         size = NY * BLOCK
@@ -514,6 +515,7 @@
     for x in SCATTER[third:2 * third]:
         scatter_inner(z, y, x, parts, land, ssem)
     c3 = spread(ary, y, asem, nh + NZ - 2, NY, lambda j: {"depth": level(z, y, 0, j)}, collect(arz, NZ, c2))
+    gather_drain(z, y, kv, gsem)
     for x in SCATTER[2 * third:]:
         scatter_inner(z, y, x, parts, land, ssem)
     gv_ref[...] = scatter_own(z, y, 1, parts, land, ssem).astype(bf16)
@@ -524,7 +526,6 @@
     kgain_ref[...] = total[1:2]
     for cp in c1 + c2 + c3:
         cp.wait_send()
-    gather_drain(z, y, kv, gsem)
     scatter_drain(z, y, parts, land, ssem)
     for cp in done:
         cp.wait()

time: 105 us -> 105 us (level)
  no operation moved by 1% of the time
where the time goes in v4:
time: 105 us
  Pallas kernels  104 us (99%)
    pallas_call x1, Pallas kernels, fused(): pl.pallas_call(functools.partial(fused_kernel, nh, LC, RT), out_shape=(sd...  102 us
    pallas_call x1, Pallas kernels, hand_on(): pl.pallas_call(hand_on_kernel, out_shape=tuple((jax.ShapeDtypeStruct(a.sh...  2.26 us

profile of v4, /device:TPU:2, one launch (start us, length us, event | category | flops | bytes accessed | tf_op | source)
XLA Modules:
  0.0 104.5 jit_solution(4721112141822081006)
XLA Ops:
  0.6 101.6 %tree_attention.1 = (bf16[256,1024]{1,0:T(8,128)(2,1)}, bf16[256,1024]{1,0:T(8,128)(2,1)}, bf16[256,128]{1,0:T(8,128)(2,1)}, bf16[256,128]{1,0:T(8,128)(2,1)}, f32[1,128]{1,0:T(1,128)}, /*index=5*/f32[1,128]{1,0:T(1,128)}) custom-call(s32[64,64]{1,0:T(8,128)} %mask_ref.1, s32[64]{0:T(128)} %count_ref.1, bf16[256,1024]{1,0:T(8,128)(2,1)} %q_ref.1, ...), custom_call_target="tpu_custom_call" | custom-call | tf_op jit(solution)/shard_map/tree_attention/pallas_call | solution.py:543
  102.3 2.3 %hand_on.1 = (bf16[256,1024]{1,0:T(8,128)(2,1)}, bf16[256,1024]{1,0:T(8,128)(2,1)}, bf16[256,128]{1,0:T(8,128)(2,1)}, bf16[256,128]{1,0:T(8,128)(2,1)}, f32[1,128]{1,0:T(1,128)}, /*index=5*/f32[1,128]{1,0:T(1,128)}) custom-call(bf16[256,1024]{1,0:T(8,128)(2,1)} %get-tuple-element.18.refs_0_, bf16[256,1024]{1,0:T(8,128)(2,1)} %get-tuple-element.19.refs_1_, ...), custom_call_target="tpu_custom_call" | custom-call | tf_op jit(solution)/shard_map/hand_on/pallas_call | solution.py:570
